TPU v7x, 32 devices: a whole 2x2x4 slice. The times are simulated.
32 devices in a mesh: grp: 2 (over x), lat: 16 (over z, y, core).
Axes of the slice: x: 2, y: 2, z: 4, core: 2. Of those that a mesh axis runs over, the one named last changes fastest.
Arguments:
- features: bfloat16 [2, 32, 192, 512], P('grp', 'lat'), parts along dimension 0, may hold values from -120 to 120
- noise_index: int32 [2], P('grp'), parts along dimension 0, may hold values from 0 to 17
- sigma_table: float32 [18], replicated, may hold values from 0.002 to 80
- affine_weight: bfloat16 [128, 1024], replicated, may hold values from -0.5 to 0.5
- norm_gain: float32 [3, 512], replicated, may hold values from 0.1 to 1.9
- norm_bias: float32 [3, 512], replicated, may hold values from -3 to 3
- conv1_weight: bfloat16 [3, 3, 512, 512], replicated, may hold values from -0.09375 to 0.09375
- conv2_weight: bfloat16 [3, 3, 512, 512], replicated, may hold values from -0.09375 to 0.09375
- conv_bias: float32 [2, 512], replicated, may hold values from -3 to 3
- qkv_weight: bfloat16 [512, 1536], replicated, may hold values from -3 to 3
- proj_weight: bfloat16 [512, 512], replicated, may hold values from -0.25 to 0.25
- proj_bias: float32 [512], replicated, may hold values from -3 to 3
Outputs:
- bottleneck: bfloat16 [2, 16, 96, 512], P('grp', 'lat'), parts along dimension 0
There are 2 independent parts, one for each index of `grp`. A program takes and returns all parts, laid end to end along the dimension named above; an argument that names none is the same for every part. Nothing has to cross between parts.
All inputs are finite; a program needn't handle non-finite values.
Results may differ from a plain program's by a relative error of at most 0.012.
The roundings to bfloat16 on the way count: a program that leaves them out, or rounds other values in their place, can miss the bound.
Values may be sent and summed in bfloat16 or wider, within the bound.
A program may use at most 128 MiB of HBM per device.

v0:
```python
import math
import jax
import jax.numpy as jnp
from jax import lax
from jax.sharding import PartitionSpec as P

HEAD_DIM = 64
GROUPS = 32
FREQS = 64
eps = 1e-05
skip_gain = 0.7071067811865476


def with_halo(block, sides, width):
    for axis, dim in sides:
        count = lax.axis_size(axis)
        forward = [(i, i + 1) for i in range(count - 1)]
        backward = [(target, source) for source, target in forward]
        low = lax.ppermute(
            lax.slice_in_dim(block, block.shape[dim] - width, None, axis=dim), axis, forward
        )
        high = lax.ppermute(lax.slice_in_dim(block, 0, width, axis=dim), axis, backward)
        block = jnp.concatenate([low, block, high], axis=dim)
    return block


def noise_terms(noise_index, sigma_table, affine_weight):
    levels_count = sigma_table.shape[0]
    chosen = (noise_index[:, None] == jnp.arange(levels_count, dtype=jnp.int32)[None, :]).astype(
        jnp.float32
    )
    sigmas = jnp.sum(chosen * sigma_table[None, :], axis=1)
    log_level = jnp.log(sigmas) / 4.0
    frequency = jnp.exp(-math.log(10000.0) * jnp.arange(FREQS, dtype=jnp.float32) / FREQS)
    angles = log_level[:, None] * frequency[None, :]
    fourier = jnp.concatenate([jnp.cos(angles), jnp.sin(angles)], axis=1).astype(jnp.bfloat16)
    affine = jnp.dot(fourier, affine_weight, preferred_element_type=jnp.float32)
    channels = affine.shape[1] // 2
    return (affine[:, :channels], affine[:, channels:])


def band_moments(values):
    members, height, breadth, channels = values.shape
    group_width = channels // GROUPS
    entries = height * breadth * group_width * lax.axis_size("lat")
    column_sums = jnp.sum(values, axis=(1, 2)).reshape(members, GROUPS, group_width).sum(axis=2)
    column_squares = (
        jnp.sum(jnp.square(values), axis=(1, 2)).reshape(members, GROUPS, group_width).sum(axis=2)
    )
    totals, squares = lax.psum((column_sums, column_squares), "lat")
    center = totals / entries
    spread = squares / entries - center * center
    return (center, spread)


def normalize(values, center, spread, norm_scale, norm_offset):
    group_width = values.shape[-1] // GROUPS
    center_full = jnp.repeat(center, group_width, axis=1)[:, None, None, :]
    factor_full = jnp.repeat(lax.rsqrt(spread + eps), group_width, axis=1)[:, None, None, :]
    return (values - center_full) * factor_full * norm_scale + norm_offset


def convolve(values, kernel):
    return lax.conv_general_dilated(
        values,
        kernel,
        (1, 1),
        ((0, 0), (1, 1)),
        dimension_numbers=("NHWC", "HWIO", "NHWC"),
        preferred_element_type=jnp.float32,
    )


def with_rims(values):
    return with_halo(values, (("lat", 1),), 1)


def key_span(total_rows, breadth):
    row_limit = max(1, 1024 // breadth)
    return math.gcd(total_rows, 1 << row_limit.bit_length() - 1)


def accumulate(running, queries, key_block, value_block):
    blended, largest, totals = running
    scores = jnp.einsum(
        "mqhd,mkhd->mqhk", queries, key_block, preferred_element_type=jnp.float32
    ) * HEAD_DIM ** (-0.5)
    rising = jnp.maximum(largest, jnp.max(scores, axis=-1))
    fading = jnp.exp(largest - rising)
    weights = jnp.exp(scores - rising[..., None])
    totals = totals * fading + jnp.sum(weights, axis=-1)
    blended = blended * fading[..., None] + jnp.einsum(
        "mqhk,mkhd->mqhd",
        weights.astype(jnp.bfloat16),
        value_block,
        preferred_element_type=jnp.float32,
    )
    return (blended, rising, totals)


def local(
    features,
    noise_index,
    sigma_table,
    affine_weight,
    norm_gain,
    norm_bias,
    conv1_weight,
    conv2_weight,
    conv_bias,
    qkv_weight,
    proj_weight,
    proj_bias,
):
    film_scale, film_shift = noise_terms(noise_index, sigma_table, affine_weight)
    film_scale = film_scale[:, None, None, :]
    film_shift = film_shift[:, None, None, :]
    source = features.astype(jnp.float32)
    center, spread = band_moments(source)
    active = jax.nn.silu(normalize(source, center, spread, norm_gain[0], norm_bias[0])).astype(
        jnp.bfloat16
    )
    first_conv = convolve(with_rims(active), conv1_weight) + conv_bias[0]
    center, spread = band_moments(first_conv)
    middle = jax.nn.silu(
        normalize(first_conv, center, spread, norm_gain[1], norm_bias[1]) * (1.0 + film_scale)
        + film_shift
    ).astype(jnp.bfloat16)
    second_conv = convolve(with_rims(middle), conv2_weight)
    level_one = ((source + second_conv + conv_bias[1]) * skip_gain).astype(jnp.bfloat16)
    level_one = lax.optimization_barrier(level_one)
    members, height, breadth, channels = level_one.shape
    low_rows = height // 2
    breadth_low = breadth // 2
    pooled = jnp.mean(
        level_one.astype(jnp.float32).reshape(members, low_rows, 2, breadth_low, 2, channels),
        axis=(2, 4),
    )
    center, spread = band_moments(pooled)
    normed = normalize(pooled, center, spread, norm_gain[2], norm_bias[2]).astype(jnp.bfloat16)
    tokens = low_rows * breadth_low
    head_count = channels // HEAD_DIM
    flat_rows = normed.reshape(members * tokens, channels)
    all_rows = low_rows * lax.axis_size("lat")
    span_rows = key_span(all_rows, breadth_low)
    span_count = all_rows // span_rows
    running = (
        jnp.zeros((members, tokens, head_count, HEAD_DIM), jnp.float32),
        jnp.full((members, tokens, head_count), -1e30, jnp.float32),
        jnp.zeros((members, tokens, head_count), jnp.float32),
    )
    projected = jnp.dot(flat_rows, qkv_weight, preferred_element_type=jnp.float32).astype(
        jnp.bfloat16
    )
    projected = projected.reshape(members, low_rows, breadth_low, 3, channels)
    queries = projected[:, :, :, 0].reshape(members, tokens, head_count, HEAD_DIM)
    key_all, value_all = (
        lax.all_gather(projected[:, :, :, 1], "lat", axis=1, tiled=True),
        lax.all_gather(projected[:, :, :, 2], "lat", axis=1, tiled=True),
    )

    def key_span_step(step_index, inner_state):
        key_slab = lax.dynamic_slice_in_dim(key_all, step_index * span_rows, span_rows, 1).reshape(
            members, span_rows * breadth_low, head_count, HEAD_DIM
        )
        value_slab = lax.dynamic_slice_in_dim(
            value_all, step_index * span_rows, span_rows, 1
        ).reshape(members, span_rows * breadth_low, head_count, HEAD_DIM)
        return accumulate(inner_state, queries, key_slab, value_slab)

    running = lax.fori_loop(0, span_count, key_span_step, running)
    blended, largest, totals = running
    attended = (
        (blended / totals[..., None]).reshape(members * tokens, channels).astype(jnp.bfloat16)
    )
    output_proj = jnp.dot(attended, proj_weight, preferred_element_type=jnp.float32) + proj_bias
    return ((pooled + output_proj.reshape(pooled.shape)) * skip_gain).astype(jnp.bfloat16)


def solution(mesh):
    return jax.shard_map(
        local,
        mesh=mesh,
        in_specs=(
            P("grp", "lat", None, None),
            P("grp"),
            P(),
            P(),
            P(),
            P(),
            P(),
            P(),
            P(),
            P(),
            P(),
            P(),
        ),
        out_specs=P("grp", "lat", None, None),
        check_vma=False,
    )
```

profile of v0, /device:TPU:0, one launch (start us, length us, event | category | flops | bytes accessed | tf_op | source)
XLA Modules:
  0.0 249.0 jit_solution(6614196855762687472)
XLA Ops:
  6.5 1.2 convert_reduce_fusion
  7.8 0.8 fusion.72
  8.6 0.8 fusion.73
  9.8 34.9 %all-reduce.2 = (f32[1,32]{1,0:T(1,128)S(1)}, f32[1,32]{1,0:T(1,128)S(1)}) all-reduce(f32[1,32]{1,0:T(1,128)S(1)} %bitcast.170, f32[1,32]{1,0:T(1,128)S(1)} %bitcast.168), channel_id=1, replica_groups=mesh['grp'=2,'lat'=16] {'lat'}, use_global_device_ids=true, to_apply=%region_5.0 | all-reduce | flops 64 | bytes 512 | tf_op jit(solution)/shard_map/psum | solution.py:50
  45.1 1.3 fusion.45
  46.4 1.3 collective-permute-start
  47.7 1.3 collective-permute-start.1
  49.6 1.3 fusion.57
  51.8 0.8 fusion.74
  52.5 1.1 fusion.58
  55.0 1.2 copy-done.7
  56.2 2.2 select_reduce_fusion.1
  58.7 30.7 %all-reduce.1 = (f32[1,32]{1,0:T(1,128)S(1)}, f32[1,32]{1,0:T(1,128)S(1)}) all-reduce(f32[1,32]{1,0:T(1,128)S(1)} %bitcast.171, f32[1,32]{1,0:T(1,128)S(1)} %bitcast.167), channel_id=1, replica_groups=mesh['grp'=2,'lat'=16] {'lat'}, use_global_device_ids=true, to_apply=%region_11.12 | all-reduce | flops 64 | bytes 512 | tf_op jit(solution)/shard_map/psum | solution.py:50
  90.6 1.3 collective-permute-start.2
  92.6 1.5 collective-permute-start.3
  94.7 1.5 collective-permute-done.3
  96.2 1.3 maximum_bitcast_fusion.1
  98.0 4.4 %convolution_select_fusion = f32[2,8,25,512]{3,1,2,0:T(8,128)S(1)} fusion(bf16[3,3,512,512]{3,2,1,0:T(8,128)(2,1)} %param.21, bf16[4,1,7,2,512]{4,2,3,0,1:T(8,128)(2,1)S(1)} %slice.92, bf16[4,1,8,25,512]{4,2,3,0,1:T(8,128)(2,1)S(1)} %copy.102, pred[8,25]{0,1:T(8,128)(4,1)S(1)} %copy-done.8), kind=kOutput, calls=%fused_computation.30 | convolution fusion | flops 1890295808 | bytes 6414536 | tf_op jit(solution)/shard_map/conv_general_dilated | solution.py:64
  104.9 34.2 %all-reduce = (f32[1,32]{1,0:T(1,128)S(1)}, f32[1,32]{1,0:T(1,128)S(1)}) all-reduce(f32[1,32]{1,0:T(1,128)S(1)} %bitcast.169, f32[1,32]{1,0:T(1,128)S(1)} %bitcast.166), channel_id=1, replica_groups=mesh['grp'=2,'lat'=16] {'lat'}, use_global_device_ids=true, to_apply=%region_20.21 | all-reduce | flops 64 | bytes 512 | tf_op jit(solution)/shard_map/psum | solution.py:50
  142.1 36.1 %all-gather.7.cloned.1.call-done = bf16[1,16,96,1,512]{4,2,3,0,1:T(8,128)(2,1)} async-done(((bf16[1,1,96,1,512]{4,2,3,0,1:T(8,128)(2,1)}), bf16[1,16,96,1,512]{4,2,3,0,1:T(8,128)(2,1)}) %all-gather.7.cloned.1.call-update) | async-done | bytes 1572880 | tf_op jit(solution)/shard_map/all_gather | solution.py:159
  178.2 40.9 %all-gather.5.cloned.1.call-done = bf16[1,16,96,1,512]{4,2,3,0,1:T(8,128)(2,1)} async-done(((bf16[1,1,96,1,512]{4,2,3,0,1:T(8,128)(2,1)}), bf16[1,16,96,1,512]{4,2,3,0,1:T(8,128)(2,1)}) %all-gather.5.cloned.1.call-update) | async-done | bytes 1572880 | tf_op jit(solution)/shard_map/all_gather | solution.py:158
  219.1 20.1 %while.18 = (s32[]{:T(128)}, f32[1,96,8,64]{1,3,2,0:T(8,128)}, f32[1,96,8]{1,2,0:T(8,128)S(1)}, f32[1,96,8]{1,2,0:T(8,128)S(1)}, bf16[1,16,96,512]{3,2,1,0:T(8,1...) while((s32[]{:T(128)}, f32[1,96,8,64]{1,3,2,0:T(8,128)}, ...), condition=%wide.region_24.25_spmd.clone, body=%wide.region_21.24_spmd.clone.sunk | while | flops 155865600 | bytes 23347460 | solution.py:171
  219.1 2.4 constant_dynamic-slice_fusion.3
  221.5 1.7 copy.121
  223.2 1.8 reshape.314
  225.7 0.9 reshape.315
  229.2 2.4 constant_dynamic-slice_fusion.3
  231.6 1.7 copy.121
  233.3 1.8 reshape.314
  235.8 0.9 reshape.315
  239.2 1.0 divide_convert_fusion
  240.2 2.0 fusion.24
  (109 shorter events, 17.0 us)
Async XLA Ops:
  6.5 132.9 %copy-start = (bf16[512,1536]{1,0:T(8,128)(2,1)S(1)}, bf16[512,1536]{1,0:T(8,128)(2,1)}, u32[]{:S(2)}) copy-start(bf16[512,1536]{1,0:T(8,128)(2,1)} %param.23) | copy-start | bytes 4718596
  6.5 171.7 %all-gather.7.cloned.1.call-start = ((), (), s32[]{:S(2)}) async-start(), calls=%async_computation.1 | async-start | bytes 1671168 | tf_op jit(solution)/shard_map/all_gather | solution.py:159
  46.4 7.3 %collective-permute-start = (bf16[1,1,192,512]{3,2,1,0:T(8,128)(2,1)S(1)}, bf16[1,1,192,512]{3,2,1,0:T(8,128)(2,1)S(1)}, u32[]{:S(2)}, u32[]{:S(2)}) collective-permute-start(bf16[1,1,192,512]{3,2,1,0:T(8,128)(2,1)S(1)} %get-tuple-element.235), channel_id=1, source_target_pairs={{0,1},{1,2},{2,3},{3,4},{4,5},{5,6},{6,7},{7,8},{8,9},{9,10},{10,1... | collective-permute-start | bytes 589832 | tf_op jit(solution)/shard_map/ppermute | solution.py:19
  47.7 6.0 %collective-permute-start.1 = (bf16[1,1,192,512]{3,2,1,0:T(8,128)(2,1)S(1)}, bf16[1,1,192,512]{3,2,1,0:T(8,128)(2,1)S(1)}, u32[]{:S(2)}, u32[]{:S(2)}) collective-permute-start(bf16[1,1,192,512]{3,2,1,0:T(8,128)(2,1)S(1)} %get-tuple-element.236), channel_id=1, source_target_pairs={{1,0},{2,1},{3,2},{4,3},{5,4},{6,5},{7,6},{8,7},{9,8},{10,9},{11,1... | collective-permute-start | bytes 589832 | tf_op jit(solution)/shard_map/ppermute | solution.py:22
  53.8 2.3 copy-start.7
  53.8 2.3 copy-start.8
  90.6 3.7 %collective-permute-start.2 = (bf16[1,1,192,512]{3,2,1,0:T(8,128)(2,1)S(1)}, bf16[1,1,192,512]{3,2,1,0:T(8,128)(2,1)S(1)}, u32[]{:S(2)}, u32[]{:S(2)}) collective-permute-start(bf16[1,1,192,512]{3,2,1,0:T(8,128)(2,1)S(1)} %slice.88), channel_id=1, source_target_pairs={{0,1},{1,2},{2,3},{3,4},{4,5},{5,6},{6,7},{7,8},{8,9},{9,10},{10,1... | collective-permute-start | bytes 589832 | tf_op jit(solution)/shard_map/ppermute | solution.py:19
  92.6 3.6 %collective-permute-start.3 = (bf16[1,1,192,512]{3,1,2,0:T(2,128)(2,1)S(1)}, bf16[1,1,192,512]{3,1,2,0:T(2,128)(2,1)S(1)}, u32[]{:S(2)}, u32[]{:S(2)}) collective-permute-start(bf16[1,1,192,512]{3,1,2,0:T(2,128)(2,1)S(1)} %slice.91), channel_id=1, source_target_pairs={{1,0},{2,1},{3,2},{4,3},{5,4},{6,5},{7,6},{8,7},{9,8},{10,9},{11,1... | collective-permute-start | bytes 589832 | tf_op jit(solution)/shard_map/ppermute | solution.py:22
  102.5 1.0 copy-start.4
  104.4 37.4 %copy-start.5 = (f32[96,512]{1,0:T(8,128)}, f32[96,512]{1,0:T(8,128)S(1)}, u32[]{:S(2)}) copy-start(f32[96,512]{1,0:T(8,128)S(1)} %reduce_sum.173) | copy-start | bytes 589828
  141.1 78.0 %all-gather.5.cloned.1.call-start = ((), (), s32[]{:S(2)}) async-start(), calls=%async_computation | async-start | bytes 1671168 | tf_op jit(solution)/shard_map/all_gather | solution.py:158
  219.1 21.1 %copy-start.6 = (f32[512]{0:T(512)S(1)}, f32[512]{0:T(512)}, u32[]{:S(2)}) copy-start(f32[512]{0:T(512)} %param.25) | copy-start | bytes 6148
  226.6 1.1 copy-start.1
  226.6 1.2 copy-start.2
  228.5 0.7 copy-start.3
  236.6 1.1 copy-start.1
  236.6 1.2 copy-start.2
  238.5 0.7 copy-start.3
Sparse Core Ops, SparseCore 0:
  141.3 36.9 all-gather.6
  180.5 38.5 all-gather.4
where the time goes:
time: 250 us; the launch traced here: 249 us
  blocking collectives  99.9 us (40%)
  waiting for transfers between devices  78.6 us (31%)
  local copies, waits for them, and re-layouts  27.8 us (11%)
  between operations  15.2 us (6%)
  matrix products  12.7 us (5%)
  other arithmetic  9.37 us (4%)
  starting transfers between devices  5.41 us (2%)
    psum x3, blocking collectives, band_moments(): totals, squares = lax.psum((column_sums, column_squares), 'lat')  99.9 us
    all_gather x1, waiting for transfers between devices, local(): lax.all_gather(projected[:, :, :, 1], 'lat', axis=1, tiled=True)  40.9 us
    all_gather x1, waiting for transfers between devices, local(): lax.all_gather(projected[:, :, :, 2], 'lat', axis=1, tiled=True)  36.1 us
    dynamic_slice x4, local copies, waits for them, and re-layouts, key_span_step(): lax.dynamic_slice_in_dim(value_all, step_index * span_rows, span_rows, 1)  8.14 us
    conv_general_dilated x2, matrix products, convolve(): lax.conv_general_dilated(values, kernel, (1, 1), ((0, 0), (1, 1)), dimens...  6.59 us
    another operation x4, local copies, waits for them, and re-layouts  5.28 us
  transfers between devices with their start and end apart: 6, of which 3 were waited for; matrix products, arithmetic and copies ran while one was open for 2% of the time, Pallas kernels for 0%

commit v1 on v0

--- a/solution.py
+++ b/solution.py
@@ -9,6 +9,18 @@
 FREQS = 64
 eps = 1e-05
 skip_gain = 0.7071067811865476
+
+
+def gather_by_bits(array, axis, dim):
+    ways, here = (lax.axis_size(axis), lax.axis_index(axis))
+    grown, reach = (array, 1)
+    while reach < ways:
+        theirs = lax.ppermute(grown, axis, [(d, d ^ reach) for d in range(ways)])
+        mine_first = jnp.concatenate([grown, theirs], axis=dim)
+        theirs_first = jnp.concatenate([theirs, grown], axis=dim)
+        grown = jnp.where(here & reach == 0, mine_first, theirs_first)
+        reach = 2 * reach
+    return grown
 
 
 def with_halo(block, sides, width):
@@ -155,7 +167,7 @@
     projected = projected.reshape(members, low_rows, breadth_low, 3, channels)
     queries = projected[:, :, :, 0].reshape(members, tokens, head_count, HEAD_DIM)
     key_all, value_all = (
-        lax.all_gather(projected[:, :, :, 1], "lat", axis=1, tiled=True),
+        gather_by_bits(projected[:, :, :, 1], "lat", 1),
         lax.all_gather(projected[:, :, :, 2], "lat", axis=1, tiled=True),
     )
 

time: 250 us -> 236 us (0.944)
  waiting for transfers between devices: 78.6 us -> 63.6 us
  other arithmetic: 9.37 us -> 12.8 us
    ppermute x0 -> x4, waiting for transfers between devices: none -> 62 us  [gather_by_bits(): theirs = lax.ppermute(grown, axis, [(d, d ^ reach) for d in range(ways)])]
    all_gather x1 -> x0, waiting for transfers between devices: 40.9 us -> none  [local(): lax.all_gather(projected[:, :, :, 1], 'lat', axis=1, tiled=True)]
    all_gather x1, waiting for transfers between devices: 36.1 us -> 0.01 us  [local(): lax.all_gather(projected[:, :, :, 2], 'lat', axis=1, tiled=True)]
    select_n x0 -> x6, other arithmetic: none -> 3.91 us  [gather_by_bits(): grown = jnp.where(here & reach == 0, mine_first, theirs_first)]
  transfers between devices with their start and end apart: 6 -> 9, of which waited for: 3 -> 5; matrix products, arithmetic and copies ran while one was open for 2% -> 3% of each run, Pallas kernels for 0% -> 0%
where the time goes in v1:
time: 236 us
  blocking collectives  100 us (42%)
  waiting for transfers between devices  63.6 us (27%)
  local copies, waits for them, and re-layouts  26.4 us (11%)
  between operations  15.3 us (6%)
  other arithmetic  12.8 us (5%)
  matrix products  11.7 us (5%)
  starting transfers between devices  5.62 us (2%)
    psum x3, blocking collectives, band_moments(): totals, squares = lax.psum((column_sums, column_squares), 'lat')  100 us
    ppermute x4, waiting for transfers between devices, gather_by_bits(): theirs = lax.ppermute(grown, axis, [(d, d ^ reach) for d in range(ways)])  62 us
    dynamic_slice x4, local copies, waits for them, and re-layouts, key_span_step(): lax.dynamic_slice_in_dim(value_all, step_index * span_rows, span_rows, 1)  8.14 us
    conv_general_dilated x2, matrix products, convolve(): lax.conv_general_dilated(values, kernel, (1, 1), ((0, 0), (1, 1)), dimens...  6.58 us
    another operation x4, local copies, waits for them, and re-layouts  5.28 us
  transfers between devices with their start and end apart: 9, of which 5 were waited for; matrix products, arithmetic and copies ran while one was open for 3% of the time, Pallas kernels for 0%

profile of v1, /device:TPU:0, one launch (start us, length us, event | category | flops | bytes accessed | tf_op | source)
XLA Modules:
  0.0 235.6 jit_solution(724710143272817583)
XLA Ops:
  6.6 1.3 convert_reduce_fusion
  7.8 0.8 fusion.73
  9.9 34.9 %all-reduce.2 = (f32[1,32]{1,0:T(1,128)S(1)}, f32[1,32]{1,0:T(1,128)S(1)}) all-reduce(f32[1,32]{1,0:T(1,128)S(1)} %bitcast.190, f32[1,32]{1,0:T(1,128)S(1)} %bitcast.188), channel_id=1, replica_groups=mesh['grp'=2,'lat'=16] {'lat'}, use_global_device_ids=true, to_apply=%region_5.0 | all-reduce | flops 64 | bytes 512 | tf_op jit(solution)/shard_map/psum | solution.py:62
  45.1 1.3 fusion.45
  46.4 1.3 collective-permute-start
  47.7 1.3 collective-permute-start.1
  52.7 1.2 copy-done.9
  53.9 2.2 select_reduce_fusion.1
  56.5 30.7 %all-reduce.1 = (f32[1,32]{1,0:T(1,128)S(1)}, f32[1,32]{1,0:T(1,128)S(1)}) all-reduce(f32[1,32]{1,0:T(1,128)S(1)} %bitcast.191, f32[1,32]{1,0:T(1,128)S(1)} %bitcast.187), channel_id=1, replica_groups=mesh['grp'=2,'lat'=16] {'lat'}, use_global_device_ids=true, to_apply=%region_11.12 | all-reduce | flops 64 | bytes 512 | tf_op jit(solution)/shard_map/psum | solution.py:62
  88.3 1.3 collective-permute-start.2
  90.3 1.5 collective-permute-start.3
  92.4 1.5 collective-permute-done.3
  93.9 1.3 maximum_bitcast_fusion.1
  95.8 4.4 %convolution_select_fusion = f32[2,8,25,512]{3,1,2,0:T(8,128)S(1)} fusion(bf16[3,3,512,512]{3,2,1,0:T(8,128)(2,1)} %param.21, bf16[4,1,7,2,512]{4,2,3,0,1:T(8,128)(2,1)S(1)} %slice.92, bf16[4,1,8,25,512]{4,2,3,0,1:T(8,128)(2,1)S(1)} %copy.101, pred[8,25]{0,1:T(8,128)(4,1)S(1)} %copy-done.11), kind=kOutput, calls=%fused_computation.31 | convolution fusion | flops 1890295808 | bytes 6414536 | tf_op jit(solution)/shard_map/conv_general_dilated | solution.py:76
  102.6 34.5 %all-reduce = (f32[1,32]{1,0:T(1,128)S(1)}, f32[1,32]{1,0:T(1,128)S(1)}) all-reduce(f32[1,32]{1,0:T(1,128)S(1)} %bitcast.189, f32[1,32]{1,0:T(1,128)S(1)} %bitcast.186), channel_id=1, replica_groups=mesh['grp'=2,'lat'=16] {'lat'}, use_global_device_ids=true, to_apply=%region_20.21 | all-reduce | flops 64 | bytes 512 | tf_op jit(solution)/shard_map/psum | solution.py:62
  139.2 1.3 collective-permute-done.4
  140.6 7.9 %collective-permute-done.5 = bf16[1,2,96,512]{3,2,1,0:T(8,128)(2,1)S(1)} collective-permute-done((bf16[1,2,96,512]{3,2,1,0:T(8,128)(2,1)S(1)}, bf16[1,2,96,512]{3,2,1,0:T(8,128)(2,1)S(1)}, u32[]{:S(2)}, u32[]{:S(2)}) %collective-permute-start.5) | collective-permute-done | bytes 196640 | tf_op jit(solution)/shard_map/ppermute | solution.py:18
  148.7 11.4 %collective-permute-done.6 = bf16[1,4,96,512]{3,2,1,0:T(8,128)(2,1)S(1)} collective-permute-done((bf16[1,4,96,512]{3,2,1,0:T(8,128)(2,1)S(1)}, bf16[1,4,96,512]{3,2,1,0:T(8,128)(2,1)S(1)}, u32[]{:S(2)}, u32[]{:S(2)}) %collective-permute-start.6) | collective-permute-done | bytes 393248 | tf_op jit(solution)/shard_map/ppermute | solution.py:18
  160.1 1.0 maximum_select_fusion.2
  161.4 41.5 %collective-permute-done.7 = bf16[1,8,96,512]{3,2,1,0:T(8,128)(2,1)} collective-permute-done((bf16[1,8,96,512]{3,2,1,0:T(8,128)(2,1)}, bf16[1,8,96,512]{3,2,1,0:T(8,128)(2,1)}, u32[]{:S(2)}, u32[]{:S(2)}) %collective-permute-start.7) | collective-permute-done | bytes 786464 | tf_op jit(solution)/shard_map/ppermute | solution.py:18
  202.9 2.8 %maximum_select_fusion = bf16[1,16,96,512]{3,2,1,0:T(8,128)(2,1)} fusion(bf16[1,8,96,512]{3,2,1,0:T(8,128)(2,1)} %collective-permute-done.7, bf16[1,8,96,512]{3,2,1,0:T(8,128)(2,1)S(1)} %fusion.50, pred[]{:T(512)S(6)} %eq.26), kind=kLoop, calls=%fused_computation.26 | loop fusion | flops 2359296 | bytes 3145729 | tf_op jit(solution)/shard_map/jit(_where)/select_n | solution.py:21
  205.7 20.1 %while.18 = (s32[]{:T(128)}, f32[1,96,8,64]{1,3,2,0:T(8,128)}, f32[1,96,8]{1,2,0:T(8,128)S(1)}, f32[1,96,8]{1,2,0:T(8,128)S(1)}, bf16[1,16,96,512]{3,2,1,0:T(8,1...) while((s32[]{:T(128)}, f32[1,96,8,64]{1,3,2,0:T(8,128)}, ...), condition=%wide.region_24.25_spmd.clone, body=%wide.region_21.24_spmd.clone.sunk | while | flops 155865600 | bytes 23347460 | solution.py:183
  205.7 2.4 %constant_dynamic-slice_fusion.3 = (bf16[1,8,96,512]{3,2,1,0:T(8,128)(2,1)}, bf16[1,8,96,512]{3,2,1,0:T(8,128)(2,1)S(1)}) fusion(bf16[1,16,96,512]{3,2,1,0:T(8,128)(2,1)} %get-tuple-element.341, s32[]{:T(128)S(6)} %select_n.153, bf16[1,16,96,512]{3,2,1,0:T(8,128)(2,1)} %get-tuple-element.339), kind=kLoop, calls=%fused_computation.19.clone.1 | loop fusion | bytes 3145732 | tf_op jit(solution)/shard_map/while/body/eval_jaxpr/dynamic_slice | solution.py:178
  208.1 1.7 copy.124
  209.8 1.8 reshape.733
  212.3 0.9 reshape.734
  215.8 2.4 %constant_dynamic-slice_fusion.3 = (bf16[1,8,96,512]{3,2,1,0:T(8,128)(2,1)}, bf16[1,8,96,512]{3,2,1,0:T(8,128)(2,1)S(1)}) fusion(bf16[1,16,96,512]{3,2,1,0:T(8,128)(2,1)} %get-tuple-element.341, s32[]{:T(128)S(6)} %select_n.153, bf16[1,16,96,512]{3,2,1,0:T(8,128)(2,1)} %get-tuple-element.339), kind=kLoop, calls=%fused_computation.19.clone.1 | loop fusion | bytes 3145732 | tf_op jit(solution)/shard_map/while/body/eval_jaxpr/dynamic_slice | solution.py:178
  218.2 1.7 copy.124
  219.8 1.8 reshape.733
  222.3 0.9 reshape.734
  225.8 1.0 divide_convert_fusion
  226.8 2.0 fusion.24
  (128 shorter events, 18.5 us)
Async XLA Ops:
  6.5 130.8 %copy-start = (bf16[512,1536]{1,0:T(8,128)(2,1)S(1)}, bf16[512,1536]{1,0:T(8,128)(2,1)}, u32[]{:S(2)}) copy-start(bf16[512,1536]{1,0:T(8,128)(2,1)} %param.23) | copy-start | bytes 4718596
  6.5 43.2 %copy-start.10 = (f32[18]{0:T(128)S(1)}, f32[18]{0:T(128)}, u32[]{:S(2)}) copy-start(f32[18]{0:T(128)} %param.16) | copy-start | bytes 220
  6.5 44.6 %copy-start.7 = (f32[2,512]{1,0:T(2,128)S(1)}, f32[2,512]{1,0:T(2,128)}, u32[]{:S(2)}) copy-start(f32[2,512]{1,0:T(2,128)} %param.22) | copy-start | bytes 12292
  6.5 44.7 %copy-start.6 = (bf16[128,1024]{1,0:T(8,128)(2,1)S(1)}, bf16[128,1024]{1,0:T(8,128)(2,1)}, u32[]{:S(2)}) copy-start(bf16[128,1024]{1,0:T(8,128)(2,1)} %param.17) | copy-start | bytes 786436
  6.5 199.1 %all-gather.3.cloned.1.call-start = ((), (), s32[]{:S(2)}) async-start(), calls=%async_computation | async-start | bytes 1671168 | tf_op jit(solution)/shard_map/all_gather | solution.py:171
  46.4 5.0 %collective-permute-start = (bf16[1,1,192,512]{3,2,1,0:T(8,128)(2,1)S(1)}, bf16[1,1,192,512]{3,2,1,0:T(8,128)(2,1)S(1)}, u32[]{:S(2)}, u32[]{:S(2)}) collective-permute-start(bf16[1,1,192,512]{3,2,1,0:T(8,128)(2,1)S(1)} %get-tuple-element.235), channel_id=1, source_target_pairs={{0,1},{1,2},{2,3},{3,4},{4,5},{5,6},{6,7},{7,8},{8,9},{9,10},{10,1... | collective-permute-start | bytes 589832 | tf_op jit(solution)/shard_map/ppermute | solution.py:31
  47.7 3.7 %collective-permute-start.1 = (bf16[1,1,192,512]{3,2,1,0:T(8,128)(2,1)S(1)}, bf16[1,1,192,512]{3,2,1,0:T(8,128)(2,1)S(1)}, u32[]{:S(2)}, u32[]{:S(2)}) collective-permute-start(bf16[1,1,192,512]{3,2,1,0:T(8,128)(2,1)S(1)} %get-tuple-element.236), channel_id=1, source_target_pairs={{1,0},{2,1},{3,2},{4,3},{5,4},{6,5},{7,6},{8,7},{9,8},{10,9},{11,1... | collective-permute-start | bytes 589832 | tf_op jit(solution)/shard_map/ppermute | solution.py:34
  51.5 2.3 copy-start.9
  52.2 1.7 copy-start.11
  88.3 3.7 %collective-permute-start.2 = (bf16[1,1,192,512]{3,2,1,0:T(8,128)(2,1)S(1)}, bf16[1,1,192,512]{3,2,1,0:T(8,128)(2,1)S(1)}, u32[]{:S(2)}, u32[]{:S(2)}) collective-permute-start(bf16[1,1,192,512]{3,2,1,0:T(8,128)(2,1)S(1)} %slice.88), channel_id=1, source_target_pairs={{0,1},{1,2},{2,3},{3,4},{4,5},{5,6},{6,7},{7,8},{8,9},{9,10},{10,1... | collective-permute-start | bytes 589832 | tf_op jit(solution)/shard_map/ppermute | solution.py:31
  90.3 3.6 %collective-permute-start.3 = (bf16[1,1,192,512]{3,1,2,0:T(2,128)(2,1)S(1)}, bf16[1,1,192,512]{3,1,2,0:T(2,128)(2,1)S(1)}, u32[]{:S(2)}, u32[]{:S(2)}) collective-permute-start(bf16[1,1,192,512]{3,1,2,0:T(2,128)(2,1)S(1)} %slice.91), channel_id=1, source_target_pairs={{1,0},{2,1},{3,2},{4,3},{5,4},{6,5},{7,6},{8,7},{9,8},{10,9},{11,1... | collective-permute-start | bytes 589832 | tf_op jit(solution)/shard_map/ppermute | solution.py:34
  100.2 1.0 copy-start.4
  102.1 36.3 %copy-start.5 = (f32[96,512]{1,0:T(8,128)}, f32[96,512]{1,0:T(8,128)S(1)}, u32[]{:S(2)}) copy-start(f32[96,512]{1,0:T(8,128)S(1)} %reduce_sum.173) | copy-start | bytes 589828
  139.1 1.4 collective-permute-start.4
  140.5 8.0 %collective-permute-start.5 = (bf16[1,2,96,512]{3,2,1,0:T(8,128)(2,1)S(1)}, bf16[1,2,96,512]{3,2,1,0:T(8,128)(2,1)S(1)}, u32[]{:S(2)}, u32[]{:S(2)}) collective-permute-start(bf16[1,2,96,512]{3,2,1,0:T(8,128)(2,1)S(1)} %maximum_select_fusion.6), channel_id=1, source_target_pairs={{0,2},{1,3},{2,0},{3,1},{4,6},{5,7},{6,4},{7,5},{8,10},{9,11},{10,... | collective-permute-start | bytes 589832 | tf_op jit(solution)/shard_map/ppermute | solution.py:18
  148.5 11.6 %collective-permute-start.6 = (bf16[1,4,96,512]{3,2,1,0:T(8,128)(2,1)S(1)}, bf16[1,4,96,512]{3,2,1,0:T(8,128)(2,1)S(1)}, u32[]{:S(2)}, u32[]{:S(2)}) collective-permute-start(bf16[1,4,96,512]{3,2,1,0:T(8,128)(2,1)S(1)} %maximum_select_fusion.4), channel_id=1, source_target_pairs={{0,4},{1,5},{2,6},{3,7},{4,0},{5,1},{6,2},{7,3},{8,12},{9,13},{10,... | collective-permute-start | bytes 1179656 | tf_op jit(solution)/shard_map/ppermute | solution.py:18
  161.1 41.8 %collective-permute-start.7 = (bf16[1,8,96,512]{3,2,1,0:T(8,128)(2,1)}, bf16[1,8,96,512]{3,2,1,0:T(8,128)(2,1)}, u32[]{:S(2)}, u32[]{:S(2)}) collective-permute-start(bf16[1,8,96,512]{3,2,1,0:T(8,128)(2,1)} %maximum_select_fusion.2), channel_id=1, source_target_pairs={{0,8},{1,9},{2,10},{3,11},{4,12},{5,13},{6,14},{7,15},{8,0},{9,1},... | collective-permute-start | bytes 2359304 | tf_op jit(solution)/shard_map/ppermute | solution.py:18
  205.7 21.1 %copy-start.8 = (f32[512]{0:T(512)S(1)}, f32[512]{0:T(512)}, u32[]{:S(2)}) copy-start(f32[512]{0:T(512)} %param.25) | copy-start | bytes 6148
  213.2 1.1 copy-start.1
  213.2 1.2 copy-start.2
  215.0 0.7 copy-start.3
  223.2 1.1 copy-start.1
  223.2 1.2 copy-start.2
  225.1 0.7 copy-start.3
Sparse Core Ops, SparseCore 0:
  139.2 65.2 all-gather.2
